TPU v7x, 512 devices: a whole 4x8x8 slice. The times are simulated.
512 devices in a mesh: ctx: 64 (over z, y_lo, core), ch: 8 (over y_hi, x).
Axes of the slice: x: 4, y: 8 (y_hi: 2, y_lo: 4; y = y_hi * 4 + y_lo), z: 8, core: 2. Of those that a mesh axis runs over, the one named last changes fastest.
Arguments:
- hidden: bfloat16 [8192, 8192], P('ctx', 'ch'), may hold values from -2000 to 2000
- gating: bfloat16 [8192, 8192], P('ctx', 'ch'), may hold values from -6 to 6
- filter_taps: bfloat16 [8192, 8192], P('ctx', 'ch'), may hold values from -181.01934 to 181.01934
- norm_gain: float32 [8192], P('ch'), may hold values from 0.25 to 1.75
- upstream: bfloat16 [8192, 8192], P('ctx', 'ch'), may hold values from -6 to 6
Outputs:
- output: bfloat16 [8192, 8192], P('ctx', 'ch')
- gate_grad: bfloat16 [8192, 8192], P('ctx', 'ch')
- filter_grad: bfloat16 [8192, 8192], P('ctx', 'ch')
- hidden_grad: bfloat16 [8192, 8192], P('ctx', 'ch')
All inputs are finite; a program needn't handle non-finite values.
Results may differ from a plain program's by a relative error of at most 0.0058.
Values may be sent and summed in bfloat16 or wider, within the bound.
A program may use at most 64 MiB of HBM per device.

v0:
```python
import functools
import math

import jax
import jax.numpy as jnp
import numpy as np
from jax import lax
from jax.experimental import pallas as pl
from jax.experimental.pallas import tpu as pltpu
from jax.sharding import PartitionSpec as P

MESH = pl.DeviceIdType.MESH
EPSILON = 1e-06
F32, BF16 = jnp.float32, jnp.bfloat16

WIDTH = 8192
CTX, CH = 64, 8
ROWS = 128
COLS = 1024
OWN = 16
LENGTH = CTX * ROWS


def split(values):
    high = values.astype(BF16)
    return high, (values - high.astype(F32)).astype(BF16)


def split_table(values):
    high = np.asarray(values, np.float32).astype(jnp.bfloat16)
    low = (np.asarray(values, np.float64) - high.astype(np.float64)).astype(jnp.bfloat16)
    return high, low


def tables():
    wave = np.arange(CTX)[:, None] + 0.25
    block = 2.0 * np.pi * wave * np.arange(CTX)[None, :] / CTX
    twist = 2.0 * np.pi * wave * np.arange(ROWS)[None, :] / LENGTH
    inner = 2.0 * np.pi * np.arange(ROWS)[:, None] * np.arange(ROWS)[None, :] / ROWS
    outer = np.concatenate([np.cos(block), -np.sin(block)], 0)
    dense = np.block([[np.cos(inner), -np.sin(inner)], [np.sin(inner), np.cos(inner)]])
    factor = 1.0 / (math.sqrt(LENGTH) * LENGTH)
    back = outer.T * factor
    outer_hi, outer_lo = split_table(outer)
    back_hi, back_lo = split_table(back)
    dense_hi, dense_lo = split_table(dense)
    turned_hi, turned_lo = split_table(dense.T)
    return (
        np.concatenate([outer_hi, outer_lo], 1),
        np.concatenate([back_hi, back_hi, back_lo], 1),
        np.stack([dense_hi, dense_lo]),
        np.stack([turned_hi, turned_lo]),
        np.stack([np.cos(twist), np.sin(twist)]).astype(np.float32),
    )


def dot(a, b):
    return jnp.dot(a, b, preferred_element_type=F32)


def kernel(
    hidden_hbm, gating_hbm, taps_hbm, upstream_hbm, gain_ref, outer_ref, back_ref, dense_ref, turned_ref, twist_ref,
    output_hbm, gate_grad_hbm, filter_grad_hbm, hidden_grad_hbm,
    hidden, gating, taps, upstream,
    output, gate_grad, filter_grad, hidden_grad,
    send, recv, spec, part_hi, part_lo, wide, stage, hidden_t, gain_t, sums, sums_in,
    load_sem, store_sem, send_sem, recv_sem, sum_send, sum_recv,
):
    me, mych = lax.axis_index("ctx"), lax.axis_index("ch")
    loads = [
        pltpu.make_async_copy(src, dst, load_sem.at[i])
        for i, (src, dst) in enumerate(
            ((taps_hbm, taps), (hidden_hbm, hidden), (upstream_hbm, upstream), (gating_hbm, gating))
        )
    ]
    for load in loads:
        load.start()

    barrier = pltpu.get_barrier_semaphore()

    def greet(i, carry):
        peer = lax.rem(me + i, CTX)
        pl.semaphore_signal(barrier, inc=1, device_id={"ctx": peer}, device_id_type=MESH)
        return carry

    def greet_ch(i, carry):
        peer = lax.rem(mych + i, CH)
        pl.semaphore_signal(barrier, inc=1, device_id={"ch": peer}, device_id_type=MESH)
        return carry

    lax.fori_loop(1, CTX, greet, 0)
    lax.fori_loop(1, CH, greet_ch, 0)

    def exchange(a):
        recv[a, me] = send[a, me]

        def one(i, carry):
            peer = lax.rem(me + i, CTX)
            pltpu.make_async_remote_copy(
                src_ref=send.at[a, peer], dst_ref=recv.at[a, me], send_sem=send_sem.at[a], recv_sem=recv_sem.at[a],
                device_id={"ctx": peer}, device_id_type=MESH,
            ).start()
            return carry

        lax.fori_loop(1, CTX, one, 0)

    def whole(a):
        rest = pl.ds(0, CTX - 1)
        return pltpu.make_async_remote_copy(
            src_ref=send.at[a, rest], dst_ref=recv.at[a, rest], send_sem=send_sem.at[a], recv_sem=recv_sem.at[a],
            device_id={"ctx": lax.rem(me + 1, CTX)}, device_id_type=MESH,
        )

    def add_up(which, partial):
        sums[which] = partial
        sums_in[which, mych] = partial

        def one(i, carry):
            peer = lax.rem(mych + i, CH)
            pltpu.make_async_remote_copy(
                src_ref=sums.at[which], dst_ref=sums_in.at[which, mych],
                send_sem=sum_send.at[which], recv_sem=sum_recv.at[which],
                device_id={"ch": peer}, device_id_type=MESH,
            ).start()
            return carry

        lax.fori_loop(1, CH, one, 0)

    def whole_sum(which):
        rest = pl.ds(0, CH - 1)
        return pltpu.make_async_remote_copy(
            src_ref=sums_in.at[which, rest], dst_ref=sums_in.at[which, rest],
            send_sem=sum_send.at[which], recv_sem=sum_recv.at[which],
            device_id={"ch": lax.rem(mych + 1, CH)}, device_id_type=MESH,
        )

    def added(which):
        whole_sum(which).wait_recv()
        total = jnp.sum(sums_in[which], axis=0)
        return jnp.sum(total, axis=0, keepdims=True) * (1.0 / WIDTH)

    def turn_out(a, block, values):
        send[a, pl.ds(block * 8, 8)] = jnp.transpose(values).reshape(8, OWN, ROWS).astype(BF16)

    def forward(a):
        stage[...] = recv[a].reshape(COLS, ROWS).astype(F32)

        def pair(p, carry):
            x = jnp.concatenate([stage[pl.ds(2 * p + j, CTX, stride=OWN), :].astype(BF16) for j in (0, 1)], 1)
            waves = dot(outer_ref[...], jnp.concatenate([x, x], 0))
            for j in (0, 1):
                re, im = waves[:CTX, j * ROWS : (j + 1) * ROWS], waves[CTX:, j * ROWS : (j + 1) * ROWS]
                q = jnp.concatenate(
                    [re * twist_ref[0] + im * twist_ref[1], im * twist_ref[0] - re * twist_ref[1]], 1
                )
                at = pl.ds(pl.multiple_of((2 * p + j) * CTX, CTX), CTX)
                part_hi[at, :], part_lo[at, :] = split(q)
            return carry

        lax.fori_loop(0, OWN // 2, pair, 0, unroll=2)

        def rows(b, carry):
            at = pl.ds(pl.multiple_of(b * 256, 256), 256)
            high = part_hi[at, :]
            spec[a, at, :] = dot(high, dense_ref[0]) + (dot(high, dense_ref[1]) + dot(part_lo[at, :], dense_ref[0]))
            return carry

        lax.fori_loop(0, COLS // 256, rows, 0)

    def inverse(a, first, second, conjugate):
        def rows(b, carry):
            at = pl.ds(pl.multiple_of(b * 128, 128), 128)
            fr, fi = spec[first, at, :ROWS], spec[first, at, ROWS:]
            sr, si = spec[second, at, :ROWS], spec[second, at, ROWS:]
            if conjugate:
                re, im = fr * sr + fi * si, fr * si - fi * sr
            else:
                re, im = fr * sr - fi * si, fr * si + fi * sr
            high, low = split(jnp.concatenate([re, im], 1))
            wide[at, :] = dot(high, turned_ref[0]) + (dot(high, turned_ref[1]) + dot(low, turned_ref[0]))
            return carry

        lax.fori_loop(0, COLS // 128, rows, 0)

        def pair(p, carry):
            u = []
            for j in (0, 1):
                at = pl.ds(pl.multiple_of((2 * p + j) * CTX, CTX), CTX)
                re, im = wide[at, :ROWS], wide[at, ROWS:]
                u.append(
                    jnp.concatenate(
                        [re * twist_ref[0] - im * twist_ref[1], re * twist_ref[1] + im * twist_ref[0]], 0
                    )
                )
            high, low = split(jnp.concatenate(u, 1))
            y = dot(back_ref[...], jnp.concatenate([high, low, high], 0))
            for j in (0, 1):
                stage[pl.ds(2 * p + j, CTX, stride=OWN), :] = y[:, j * ROWS : (j + 1) * ROWS]
            return carry

        lax.fori_loop(0, OWN // 2, pair, 0, unroll=2)
        send[a] = stage[...].reshape(CTX, OWN, ROWS).astype(BF16)

    blocks = [slice(i * 128, (i + 1) * 128) for i in range(COLS // 128)]

    loads[0].wait()
    for i, at in enumerate(blocks):
        turn_out(0, i, taps[:, at].astype(F32))
    pl.semaphore_wait(barrier, CTX - 1 + CH - 1)
    exchange(0)

    loads[1].wait()
    partial = jnp.zeros((8, ROWS), F32)
    for at in blocks:
        turned = jnp.transpose(hidden[:, at].astype(F32))
        hidden_t[at, :] = turned
        partial = partial + jnp.sum((turned * turned).reshape(16, 8, ROWS), axis=0)
    add_up(0, partial)

    loads[2].wait()
    loads[3].wait()
    for i, at in enumerate(blocks):
        turn_out(1, i, upstream[:, at].astype(F32) * gating[:, at].astype(F32))
    exchange(1)

    for at in blocks:
        gain_t[at, :] = jnp.transpose(jnp.broadcast_to(gain_ref[:, at], (ROWS, 128)))
    inverse_rms = lax.rsqrt(added(0) + EPSILON)
    for i, at in enumerate(blocks):
        normed = hidden_t[at, :] * inverse_rms
        hidden_t[at, :] = normed
        send[2, pl.ds(i * 8, 8)] = (normed * gain_t[at, :]).astype(BF16).reshape(8, OWN, ROWS)
    exchange(2)

    whole(0).wait_recv()
    forward(0)
    whole(1).wait_recv()
    forward(1)
    inverse(3, 0, 1, True)
    exchange(3)
    whole(2).wait_recv()
    forward(2)
    inverse(4, 2, 0, False)
    exchange(4)
    inverse(5, 2, 1, True)
    exchange(5)

    whole(3).wait_recv()
    partial = jnp.zeros((8, ROWS), F32)
    for i, at in enumerate(blocks):
        scaled = recv[3, pl.ds(i * 8, 8)].astype(F32).reshape(128, ROWS) * gain_t[at, :]
        gain_t[at, :] = scaled
        partial = partial + jnp.sum((scaled * hidden_t[at, :]).reshape(16, 8, ROWS), axis=0)
    add_up(1, partial)

    stores = [
        pltpu.make_async_copy(src, dst, store_sem.at[i])
        for i, (src, dst) in enumerate(
            (
                (output, output_hbm),
                (gate_grad, gate_grad_hbm),
                (filter_grad, filter_grad_hbm),
                (hidden_grad, hidden_grad_hbm),
            )
        )
    ]
    projection = added(1)
    for at in blocks:
        value = inverse_rms * (gain_t[at, :] - hidden_t[at, :] * projection)
        hidden_grad[:, at] = jnp.transpose(value).astype(BF16)
    stores[3].start()

    whole(4).wait_recv()
    for i, at in enumerate(blocks):
        value = jnp.transpose(recv[4, pl.ds(i * 8, 8)].astype(F32).reshape(128, ROWS))
        output[:, at] = (gating[:, at].astype(F32) * value).astype(BF16)
        gate_grad[:, at] = (upstream[:, at].astype(F32) * value).astype(BF16)
    stores[0].start()
    stores[1].start()

    whole(5).wait_recv()
    for i, at in enumerate(blocks):
        filter_grad[:, at] = jnp.transpose(recv[5, pl.ds(i * 8, 8)].astype(F32).reshape(128, ROWS)).astype(BF16)
    stores[2].start()

    for a in range(6):
        whole(a).wait_send()
    for which in (0, 1):
        whole_sum(which).wait_send()
    for store in stores:
        store.wait()


def shards(hidden, gating, filter_taps, norm_gain, upstream):
    consts = [jnp.asarray(t) for t in tables()]
    whole_array = jax.ShapeDtypeStruct((ROWS, COLS), BF16)
    vmem, hbm = pl.BlockSpec(memory_space=pltpu.VMEM), pl.BlockSpec(memory_space=pl.ANY)
    block = pltpu.VMEM((ROWS, COLS), BF16)
    return pl.pallas_call(
        kernel,
        out_shape=(whole_array,) * 4,
        in_specs=[hbm] * 4 + [vmem] * 6,
        out_specs=(hbm,) * 4,
        scratch_shapes=[block] * 8
        + [
            pltpu.VMEM((6, CTX, OWN, ROWS), BF16),
            pltpu.VMEM((6, CTX, OWN, ROWS), BF16),
            pltpu.VMEM((3, COLS, 2 * ROWS), F32),
            pltpu.VMEM((COLS, 2 * ROWS), BF16),
            pltpu.VMEM((COLS, 2 * ROWS), BF16),
            pltpu.VMEM((COLS, 2 * ROWS), F32),
            pltpu.VMEM((COLS, ROWS), F32),
            pltpu.VMEM((COLS, ROWS), F32),
            pltpu.VMEM((COLS, ROWS), F32),
            pltpu.VMEM((2, 8, ROWS), F32),
            pltpu.VMEM((2, CH, 8, ROWS), F32),
            pltpu.SemaphoreType.DMA((4,)),
            pltpu.SemaphoreType.DMA((4,)),
            pltpu.SemaphoreType.DMA((6,)),
            pltpu.SemaphoreType.DMA((6,)),
            pltpu.SemaphoreType.DMA((2,)),
            pltpu.SemaphoreType.DMA((2,)),
        ],
        compiler_params=pltpu.CompilerParams(collective_id=0, has_side_effects=True, vmem_limit_bytes=40 << 20),
    )(hidden, gating, filter_taps, upstream, norm_gain.reshape(1, COLS), *consts)


def solution(mesh):
    spec = P("ctx", "ch")
    return jax.shard_map(
        shards, mesh=mesh, in_specs=(spec, spec, spec, P("ch"), spec), out_specs=(spec,) * 4, check_vma=False
    )
```

profile of v0, /device:TPU:1, one launch (start us, length us, event | category | flops | bytes accessed | tf_op | source)
XLA Modules:
  0.0 74.6 jit_solution(17839619672469805176)
XLA Ops:
  0.6 0.0 copy-start
  0.6 0.9 %copy-done = bf16[128,1024]{1,0:T(8,128)(2,1)S(1)} copy-done((bf16[128,1024]{1,0:T(8,128)(2,1)S(1)}, bf16[128,1024]{1,0:T(8,128)(2,1)}, u32[]{:S(2)}) %copy-start) | copy-done | bytes 262168
  1.6 0.0 copy-start.1
  1.6 0.9 %copy-done.1 = bf16[128,1024]{1,0:T(8,128)(2,1)S(1)} copy-done((bf16[128,1024]{1,0:T(8,128)(2,1)S(1)}, bf16[128,1024]{1,0:T(8,128)(2,1)}, u32[]{:S(2)}) %copy-start.1) | copy-done | bytes 262168
  2.5 0.0 copy-start.2
  2.5 0.9 %copy-done.2 = bf16[128,1024]{1,0:T(8,128)(2,1)S(1)} copy-done((bf16[128,1024]{1,0:T(8,128)(2,1)S(1)}, bf16[128,1024]{1,0:T(8,128)(2,1)}, u32[]{:S(2)}) %copy-start.2) | copy-done | bytes 262168
  3.5 0.0 copy-start.3
  3.5 0.9 %copy-done.3 = bf16[128,1024]{1,0:T(8,128)(2,1)S(1)} copy-done((bf16[128,1024]{1,0:T(8,128)(2,1)S(1)}, bf16[128,1024]{1,0:T(8,128)(2,1)}, u32[]{:S(2)}) %copy-start.3) | copy-done | bytes 262168
  4.4 0.0 copy-start.4
  4.4 0.9 %copy-done.4 = bf16[2,256,256]{2,1,0:T(8,128)(2,1)S(1)} copy-done((bf16[2,256,256]{2,1,0:T(8,128)(2,1)S(1)}, bf16[2,256,256]{2,1,0:T(8,128)(2,1)}, u32[]{:S(2)}) %copy-start.4) | copy-done | bytes 262168
  5.4 0.0 copy-start.5
  5.4 0.9 %copy-done.5 = bf16[2,256,256]{2,1,0:T(8,128)(2,1)S(1)} copy-done((bf16[2,256,256]{2,1,0:T(8,128)(2,1)S(1)}, bf16[2,256,256]{2,1,0:T(8,128)(2,1)}, u32[]{:S(2)}) %copy-start.5) | copy-done | bytes 262168
  6.3 0.0 copy-start.6
  6.3 0.8 %copy-done.6 = f32[2,64,128]{2,1,0:T(8,128)S(1)} copy-done((f32[2,64,128]{2,1,0:T(8,128)S(1)}, f32[2,64,128]{2,1,0:T(8,128)}, u32[]{:S(2)}) %copy-start.6) | copy-done | bytes 65560
  7.2 0.0 copy-start.7
  7.2 0.8 %copy-done.7 = bf16[64,384]{1,0:T(8,128)(2,1)S(1)} copy-done((bf16[64,384]{1,0:T(8,128)(2,1)S(1)}, bf16[64,384]{1,0:T(8,128)(2,1)}, u32[]{:S(2)}) %copy-start.7) | copy-done | bytes 49176
  8.0 0.0 copy-start.8
  8.0 0.8 %copy-done.8 = bf16[128,128]{1,0:T(8,128)(2,1)S(1)} copy-done((bf16[128,128]{1,0:T(8,128)(2,1)S(1)}, bf16[128,128]{1,0:T(8,128)(2,1)}, u32[]{:S(2)}) %copy-start.8) | copy-done | bytes 32792
  8.7 0.7 copy-done.9
  9.4 62.4 %shard_map.129 = (bf16[128,1024]{1,0:T(8,128)(2,1)S(1)}, bf16[128,1024]{1,0:T(8,128)(2,1)S(1)}, bf16[128,1024]{1,0:T(8,128)(2,1)S(1)}, bf16[128,1024]{1,0:T(8,128)(2,1)S(1)}) custom-call(bf16[128,1024]{1,0:T(8,128)(2,1)S(1)} %copy-done, bf16[128,1024]{1,0:T(8,128)(2,1)S(1)} %copy-done.1, bf16[128,1024]{1,0:T(8,128)(2,1)S(1)} %copy-done.2, ...), custom_call_target="tpu_custom_call" | custom-call | tf_op jit(solution)/shard_map/pallas_call | solution.py:299
  71.8 0.7 copy.18
  72.5 0.7 copy.19
  73.2 0.7 copy.20
  73.9 0.7 copy.21
  (1 shorter events, 0.0 us)
Async XLA Ops:
  0.6 1.0 %copy-start = (bf16[128,1024]{1,0:T(8,128)(2,1)S(1)}, bf16[128,1024]{1,0:T(8,128)(2,1)}, u32[]{:S(2)}) copy-start(bf16[128,1024]{1,0:T(8,128)(2,1)} %hidden_hbm.1) | copy-start | bytes 786436
  1.6 0.9 %copy-start.1 = (bf16[128,1024]{1,0:T(8,128)(2,1)S(1)}, bf16[128,1024]{1,0:T(8,128)(2,1)}, u32[]{:S(2)}) copy-start(bf16[128,1024]{1,0:T(8,128)(2,1)} %gating_hbm.1) | copy-start | bytes 786436
  2.5 0.9 %copy-start.2 = (bf16[128,1024]{1,0:T(8,128)(2,1)S(1)}, bf16[128,1024]{1,0:T(8,128)(2,1)}, u32[]{:S(2)}) copy-start(bf16[128,1024]{1,0:T(8,128)(2,1)} %taps_hbm.1) | copy-start | bytes 786436
  3.5 0.9 %copy-start.3 = (bf16[128,1024]{1,0:T(8,128)(2,1)S(1)}, bf16[128,1024]{1,0:T(8,128)(2,1)}, u32[]{:S(2)}) copy-start(bf16[128,1024]{1,0:T(8,128)(2,1)} %upstream_hbm.1) | copy-start | bytes 786436
  4.4 0.9 %copy-start.4 = (bf16[2,256,256]{2,1,0:T(8,128)(2,1)S(1)}, bf16[2,256,256]{2,1,0:T(8,128)(2,1)}, u32[]{:S(2)}) copy-start(bf16[2,256,256]{2,1,0:T(8,128)(2,1)} %constant.13.clone.turned_ref) | copy-start | bytes 786436
  5.4 0.9 %copy-start.5 = (bf16[2,256,256]{2,1,0:T(8,128)(2,1)S(1)}, bf16[2,256,256]{2,1,0:T(8,128)(2,1)}, u32[]{:S(2)}) copy-start(bf16[2,256,256]{2,1,0:T(8,128)(2,1)} %constant.12.clone.dense_ref) | copy-start | bytes 786436
  6.3 0.8 %copy-start.6 = (f32[2,64,128]{2,1,0:T(8,128)S(1)}, f32[2,64,128]{2,1,0:T(8,128)}, u32[]{:S(2)}) copy-start(f32[2,64,128]{2,1,0:T(8,128)} %constant.14.clone.twist_ref) | copy-start | bytes 196612
  7.2 0.8 %copy-start.7 = (bf16[64,384]{1,0:T(8,128)(2,1)S(1)}, bf16[64,384]{1,0:T(8,128)(2,1)}, u32[]{:S(2)}) copy-start(bf16[64,384]{1,0:T(8,128)(2,1)} %constant.11.clone.back_ref) | copy-start | bytes 147460
  8.0 0.8 %copy-start.8 = (bf16[128,128]{1,0:T(8,128)(2,1)S(1)}, bf16[128,128]{1,0:T(8,128)(2,1)}, u32[]{:S(2)}) copy-start(bf16[128,128]{1,0:T(8,128)(2,1)} %constant.10.clone.outer_ref) | copy-start | bytes 98308
  8.7 0.7 copy-start.9
where the time goes:
time: 75.1 us; the launch traced here: 74.6 us
  Pallas kernels  62.4 us (83%)
  local copies, waits for them, and re-layouts  11.6 us (15%)
    pallas_call x1, Pallas kernels, shards(): pl.pallas_call(kernel, out_shape=(whole_array,) * 4, in_specs=[hbm] * 4 +...  62.4 us
    unnamed x24, local copies, waits for them, and re-layouts  11.6 us

commit v1 on v0

v1 whole, which is shorter than its diff:
```python
import functools
import math

import jax
import jax.numpy as jnp
import numpy as np
from jax import lax
from jax.experimental import pallas as pl
from jax.experimental.pallas import tpu as pltpu
from jax.sharding import PartitionSpec as P

MESH = pl.DeviceIdType.MESH
EPSILON = 1e-06
F32, BF16 = jnp.float32, jnp.bfloat16

WIDTH = 8192
CTX, CH = 64, 8
ROWS = 128
COLS = 1024
OWN = 16
PLANE, PLANES = 8, 8
LENGTH = CTX * ROWS
VMEM_BYTES = 56 << 20


def split(values):
    high = values.astype(BF16)
    return high, (values - high.astype(F32)).astype(BF16)


def tables():
    wave = np.arange(CTX)[:, None] + 0.25
    block = 2.0 * np.pi * wave * np.arange(CTX)[None, :] / CTX
    twist = 2.0 * np.pi * wave * np.arange(ROWS)[None, :] / LENGTH
    inner = 2.0 * np.pi * np.arange(ROWS)[:, None] * np.arange(ROWS)[None, :] / ROWS
    outer = np.concatenate([np.cos(block), -np.sin(block)], 0)
    dense = np.block([[np.cos(inner), -np.sin(inner)], [np.sin(inner), np.cos(inner)]])
    factor = 1.0 / (math.sqrt(LENGTH) * LENGTH)
    back = outer.T * factor
    twisted = np.stack([np.cos(twist), np.sin(twist)])
    return [t.astype(np.float32) for t in (outer, back, dense, dense.T, twisted)]


def dot(a, b):
    return jnp.dot(a, b, preferred_element_type=F32)


def kernel(
    hidden_hbm, gating_hbm, taps_hbm, upstream_hbm, gain_hbm, outer_hbm, back_hbm, dense_hbm, turned_hbm, twist_hbm,
    output, gate_grad, filter_grad, hidden_grad,
    hidden, gating, taps, upstream, gain_ref, outer_f32, back_f32, dense_f32, turned_f32, twist_ref,
    outer_ref, back_ref, dense_ref, turned_ref,
    send, recv, spec, part_hi, part_lo, wide, stage, hidden_t, gain_t, sums, sums_in,
    load_sem, send_sem, recv_sem, sum_send, sum_recv,
):
    me, mych = lax.axis_index("ctx"), lax.axis_index("ch")
    plane, place = me // PLANE, lax.rem(me, PLANE)
    loads = [
        pltpu.make_async_copy(src, dst, load_sem.at[i])
        for i, (src, dst) in enumerate(
            (
                (taps_hbm, taps), (hidden_hbm, hidden), (upstream_hbm, upstream), (gating_hbm, gating),
                (gain_hbm, gain_ref), (outer_hbm, outer_f32), (back_hbm, back_f32),
                (dense_hbm, dense_f32), (turned_hbm, turned_f32), (twist_hbm, twist_ref),
            )
        )
    ]
    loads[0].start()

    def far_plane(i):
        step = PLANES // 2 + jnp.where(lax.rem(i, 2) == 1, -((i + 1) // 2), i // 2)
        return lax.rem(plane + step, PLANES)

    barrier = pltpu.get_barrier_semaphore()

    def greet(peer):
        pl.semaphore_signal(barrier, inc=1, device_id={"ctx": peer}, device_id_type=MESH)

    def greet_plane(i, carry):
        for j in range(PLANE):
            greet(far_plane(i) * PLANE + j)
        return carry

    lax.fori_loop(0, PLANES - 1, greet_plane, 0)
    for i in range(1, PLANE):
        greet(plane * PLANE + lax.rem(place + i, PLANE))
    for i in range(1, CH):
        peer = lax.rem(mych + i, CH)
        pl.semaphore_signal(barrier, inc=1, device_id={"ch": peer}, device_id_type=MESH)
    for load in loads[1:]:
        load.start()

    def exchange(a, fill):
        def one(to, peer):
            pltpu.make_async_remote_copy(
                src_ref=send.at[a, peer], dst_ref=recv.at[a, me],
                send_sem=send_sem.at[a], recv_sem=recv_sem.at[a, plane],
                device_id={"ctx": peer}, device_id_type=MESH,
            ).start()

        def there(i, carry):
            to = far_plane(i)
            fill(to)
            for j in range(PLANE):
                one(to, to * PLANE + lax.rem(place + j, PLANE))
            return carry

        lax.fori_loop(0, PLANES - 1, there, 0)
        fill(plane)
        for j in range(1, PLANE):
            one(plane, plane * PLANE + lax.rem(place + j, PLANE))
        recv[a, me] = send[a, me]

    def arrivals(a, use):
        def wait(at, sem):
            pltpu.make_async_remote_copy(
                src_ref=send.at[a, at], dst_ref=recv.at[a, at], send_sem=send_sem.at[a], recv_sem=sem,
                device_id={"ctx": lax.rem(me + 1, CTX)}, device_id_type=MESH,
            ).wait_recv()

        def there(i, carry):
            source = far_plane(i)
            wait(pl.ds(source * PLANE, PLANE), recv_sem.at[a, source])
            use(source)
            return carry

        lax.fori_loop(0, PLANES - 1, there, 0)
        wait(pl.ds(0, PLANE - 1), recv_sem.at[a, plane])
        use(plane)

    def sent(a):
        rest = pl.ds(0, CTX - 1)
        pltpu.make_async_remote_copy(
            src_ref=send.at[a, rest], dst_ref=recv.at[a, rest], send_sem=send_sem.at[a], recv_sem=recv_sem.at[a, 0],
            device_id={"ctx": lax.rem(me + 1, CTX)}, device_id_type=MESH,
        ).wait_send()

    def add_up(which, partial):
        sums[which] = partial
        sums_in[which, mych] = partial

        def one(i, carry):
            peer = lax.rem(mych + i, CH)
            pltpu.make_async_remote_copy(
                src_ref=sums.at[which], dst_ref=sums_in.at[which, mych],
                send_sem=sum_send.at[which], recv_sem=sum_recv.at[which],
                device_id={"ch": peer}, device_id_type=MESH,
            ).start()
            return carry

        lax.fori_loop(1, CH, one, 0)

    def whole_sum(which):
        rest = pl.ds(0, CH - 1)
        return pltpu.make_async_remote_copy(
            src_ref=sums_in.at[which, rest], dst_ref=sums_in.at[which, rest],
            send_sem=sum_send.at[which], recv_sem=sum_recv.at[which],
            device_id={"ch": lax.rem(mych + 1, CH)}, device_id_type=MESH,
        )

    def added(which):
        whole_sum(which).wait_recv()
        total = jnp.sum(sums_in[which], axis=0)
        return jnp.sum(total, axis=0, keepdims=True) * (1.0 / WIDTH)

    def part(block):
        return pl.ds(pl.multiple_of(block * 128, 128), 128), pl.ds(block * PLANE, PLANE)

    def turn_out(a, block, values):
        send[a, part(block)[1]] = jnp.transpose(values).reshape(PLANE, OWN, ROWS).astype(BF16)

    def turn_in(a, block):
        return recv[a, part(block)[1]].astype(F32).reshape(128, ROWS)

    def to_stage(a):
        def use(block):
            stage[part(block)[0], :] = turn_in(a, block)

        return use

    def from_stage(a):
        def fill(block):
            send[a, part(block)[1]] = stage[part(block)[0], :].reshape(PLANE, OWN, ROWS).astype(BF16)

        return fill

    def forward(a):
        for p in range(OWN // 2):
            x = jnp.concatenate([stage[pl.ds(2 * p + j, CTX, stride=OWN), :].astype(BF16) for j in (0, 1)], 1)
            waves = dot(outer_ref[...], jnp.concatenate([x, x], 0))
            for j in (0, 1):
                re, im = waves[:CTX, j * ROWS : (j + 1) * ROWS], waves[CTX:, j * ROWS : (j + 1) * ROWS]
                q = jnp.concatenate(
                    [re * twist_ref[0] + im * twist_ref[1], im * twist_ref[0] - re * twist_ref[1]], 1
                )
                at = pl.ds((2 * p + j) * CTX, CTX)
                part_hi[at, :], part_lo[at, :] = split(q)
        for b in range(COLS // 256):
            at = pl.ds(b * 256, 256)
            high = part_hi[at, :]
            spec[a, at, :] = dot(high, dense_ref[0]) + (dot(high, dense_ref[1]) + dot(part_lo[at, :], dense_ref[0]))

    def inverse(first, second, conjugate):
        for b in range(COLS // 256):
            at = pl.ds(b * 256, 256)
            fr, fi = spec[first, at, :ROWS], spec[first, at, ROWS:]
            sr, si = spec[second, at, :ROWS], spec[second, at, ROWS:]
            if conjugate:
                re, im = fr * sr + fi * si, fr * si - fi * sr
            else:
                re, im = fr * sr - fi * si, fr * si + fi * sr
            high, low = split(jnp.concatenate([re, im], 1))
            wide[at, :] = dot(high, turned_ref[0]) + (dot(high, turned_ref[1]) + dot(low, turned_ref[0]))
        for p in range(OWN // 2):
            u = []
            for j in (0, 1):
                at = pl.ds((2 * p + j) * CTX, CTX)
                re, im = wide[at, :ROWS], wide[at, ROWS:]
                u.append(
                    jnp.concatenate(
                        [re * twist_ref[0] - im * twist_ref[1], re * twist_ref[1] + im * twist_ref[0]], 0
                    )
                )
            high, low = split(jnp.concatenate(u, 1))
            y = dot(back_ref[...], jnp.concatenate([high, low, high], 0))
            for j in (0, 1):
                stage[pl.ds(2 * p + j, CTX, stride=OWN), :] = y[:, j * ROWS : (j + 1) * ROWS]

    blocks = range(COLS // 128)

    loads[0].wait()
    for i in blocks:
        turn_out(0, i, taps[:, part(i)[0]].astype(F32))
    pl.semaphore_wait(barrier, CTX - 1 + CH - 1)
    exchange(0, lambda block: None)

    loads[1].wait()
    partial = jnp.zeros((8, ROWS), F32)
    for i in blocks:
        turned = jnp.transpose(hidden[:, part(i)[0]].astype(F32))
        hidden_t[part(i)[0], :] = turned
        partial = partial + jnp.sum((turned * turned).reshape(16, 8, ROWS), axis=0)
    add_up(0, partial)

    loads[2].wait()
    loads[3].wait()

    def conv_grad(block):
        at = part(block)[0]
        turn_out(1, block, upstream[:, at].astype(F32) * gating[:, at].astype(F32))

    exchange(1, conv_grad)

    loads[4].wait()
    for i in blocks:
        at = part(i)[0]
        gain_t[at, :] = jnp.transpose(jnp.broadcast_to(gain_ref[:, at], (ROWS, 128)))
    inverse_rms = lax.rsqrt(added(0) + EPSILON)

    def mixed(block):
        at, owners = part(block)
        normed = hidden_t[at, :] * inverse_rms
        hidden_t[at, :] = normed
        send[2, owners] = (normed * gain_t[at, :]).astype(BF16).reshape(PLANE, OWN, ROWS)

    exchange(2, mixed)

    for load in loads[5:]:
        load.wait()
    high, low = split(outer_f32[...])
    outer_ref[...] = jnp.concatenate([high, low], 1)
    high, low = split(back_f32[...])
    back_ref[...] = jnp.concatenate([high, high, low], 1)
    dense_ref[0], dense_ref[1] = split(dense_f32[...])
    turned_ref[0], turned_ref[1] = split(turned_f32[...])

    arrivals(0, to_stage(0))
    forward(0)
    arrivals(1, to_stage(1))
    forward(1)
    inverse(0, 1, True)
    exchange(3, from_stage(3))
    arrivals(2, to_stage(2))
    forward(2)
    inverse(2, 0, False)
    exchange(4, from_stage(4))
    inverse(2, 1, True)
    exchange(5, from_stage(5))

    sums[1] = jnp.zeros((8, ROWS), F32)

    def project(block):
        at = part(block)[0]
        scaled = turn_in(3, block) * gain_t[at, :]
        gain_t[at, :] = scaled
        sums[1] = sums[1] + jnp.sum((scaled * hidden_t[at, :]).reshape(16, 8, ROWS), axis=0)

    arrivals(3, project)
    add_up(1, sums[1])
    projection = added(1)
    for i in blocks:
        at = part(i)[0]
        value = inverse_rms * (gain_t[at, :] - hidden_t[at, :] * projection)
        hidden_grad[:, at] = jnp.transpose(value).astype(BF16)

    def gated(block):
        at = part(block)[0]
        value = jnp.transpose(turn_in(4, block))
        output[:, at] = (gating[:, at].astype(F32) * value).astype(BF16)
        gate_grad[:, at] = (upstream[:, at].astype(F32) * value).astype(BF16)

    arrivals(4, gated)

    def taps_grad(block):
        filter_grad[:, part(block)[0]] = jnp.transpose(turn_in(5, block)).astype(BF16)

    arrivals(5, taps_grad)

    for a in range(6):
        sent(a)
    for which in (0, 1):
        whole_sum(which).wait_send()


def finish(*refs):
    copies = [pltpu.make_async_copy(refs[i], refs[4 + i], refs[8].at[i]) for i in range(4)]
    for copy in copies:
        copy.start()
    for copy in copies:
        copy.wait()


def shards(hidden, gating, filter_taps, norm_gain, upstream):
    consts = [jnp.asarray(t) for t in tables()]
    vmem, hbm = pl.BlockSpec(memory_space=pltpu.VMEM), pl.BlockSpec(memory_space=pltpu.HBM)
    block = pltpu.VMEM((ROWS, COLS), BF16)
    gain = norm_gain.reshape(1, COLS)
    results = pl.pallas_call(
        kernel,
        out_shape=(pltpu.VMEM((ROWS, COLS), BF16),) * 4,
        in_specs=[hbm] * 10,
        out_specs=(vmem,) * 4,
        scratch_shapes=[block] * 4
        + [pltpu.VMEM(t.shape, t.dtype) for t in (gain, *consts)]
        + [
            pltpu.VMEM((2 * CTX, 2 * CTX), BF16),
            pltpu.VMEM((CTX, 6 * CTX), BF16),
            pltpu.VMEM((2, 2 * ROWS, 2 * ROWS), BF16),
            pltpu.VMEM((2, 2 * ROWS, 2 * ROWS), BF16),
            pltpu.VMEM((6, CTX, OWN, ROWS), BF16),
            pltpu.VMEM((6, CTX, OWN, ROWS), BF16),
            pltpu.VMEM((3, COLS, 2 * ROWS), F32),
            pltpu.VMEM((COLS, 2 * ROWS), BF16),
            pltpu.VMEM((COLS, 2 * ROWS), BF16),
            pltpu.VMEM((COLS, 2 * ROWS), F32),
            pltpu.VMEM((COLS, ROWS), F32),
            pltpu.VMEM((COLS, ROWS), F32),
            pltpu.VMEM((COLS, ROWS), F32),
            pltpu.VMEM((2, 8, ROWS), F32),
            pltpu.VMEM((2, CH, 8, ROWS), F32),
            pltpu.SemaphoreType.DMA((10,)),
            pltpu.SemaphoreType.DMA((6,)),
            pltpu.SemaphoreType.DMA((6, PLANES)),
            pltpu.SemaphoreType.DMA((2,)),
            pltpu.SemaphoreType.DMA((2,)),
        ],
        compiler_params=pltpu.CompilerParams(collective_id=0, has_side_effects=True, vmem_limit_bytes=VMEM_BYTES),
    )(hidden, gating, filter_taps, upstream, gain, *consts)
    return pl.pallas_call(
        finish,
        out_shape=(pltpu.HBM((ROWS, COLS), BF16),) * 4,
        in_specs=[vmem] * 4,
        out_specs=(hbm,) * 4,
        scratch_shapes=[pltpu.SemaphoreType.DMA((4,))],
        compiler_params=pltpu.CompilerParams(vmem_limit_bytes=1 << 20),
    )(*results)


def solution(mesh):
    spec = P("ctx", "ch")
    return jax.shard_map(
        shards, mesh=mesh, in_specs=(spec, spec, spec, P("ch"), spec), out_specs=(spec,) * 4, check_vma=False
    )
```

time: 75.1 us -> 61.6 us (0.82)
  local copies, waits for them, and re-layouts: 11.6 us -> 0 us
  Pallas kernels: 62.4 us -> 60.8 us
    unnamed x24 -> x0, local copies, waits for them, and re-layouts: 11.6 us -> none
    pallas_call x1 -> x2, Pallas kernels: 62.4 us -> 60.8 us  [the longest x1 59.8 us: shards(): pl.pallas_call(kernel, out_shape=(pltpu.VMEM((ROWS, COLS), BF16),) * 4, i...]
where the time goes in v1:
time: 61.6 us; the launch traced here: 61.5 us
  Pallas kernels  60.8 us (99%)
  between operations  0.64 us (1%)
    pallas_call x1, Pallas kernels, shards(): pl.pallas_call(kernel, out_shape=(pltpu.VMEM((ROWS, COLS), BF16),) * 4, i...  59.8 us

profile of v1, /device:TPU:1, one launch (start us, length us, event | category | flops | bytes accessed | tf_op | source)
XLA Modules:
  0.0 61.5 jit_solution(3187190911300166047)
XLA Ops:
  0.6 59.8 %shard_map.129 = (bf16[128,1024]{1,0:T(8,128)(2,1)S(1)}, bf16[128,1024]{1,0:T(8,128)(2,1)S(1)}, bf16[128,1024]{1,0:T(8,128)(2,1)S(1)}, bf16[128,1024]{1,0:T(8,128)(2,1)S(1)}) custom-call(bf16[128,1024]{1,0:T(8,128)(2,1)} %hidden_hbm.1, bf16[128,1024]{1,0:T(8,128)(2,1)} %gating_hbm.1, bf16[128,1024]{1,0:T(8,128)(2,1)} %taps_hbm.1, ...), custom_call_target="tpu_custom_call" | custom-call | tf_op jit(solution)/shard_map/pallas_call | solution.py:338
  60.5 1.0 %shard_map.130 = (bf16[128,1024]{1,0:T(8,128)(2,1)}, bf16[128,1024]{1,0:T(8,128)(2,1)}, bf16[128,1024]{1,0:T(8,128)(2,1)}, bf16[128,1024]{1,0:T(8,128)(2,1)}) custom-call(bf16[128,1024]{1,0:T(8,128)(2,1)S(1)} %get-tuple-element.8.refs_0_, bf16[128,1024]{1,0:T(8,128)(2,1)S(1)} %get-tuple-element.9.refs_1_, bf16[128,1024]{1,0:T(8,128)(2,1)S(1)} %get-tuple-element.10.refs_2_, ...), custom_call_target="tpu_custom_call" | custom-call | tf_op jit(solution)/shard_map/pallas_call | solution.py:369

commit v2 on v1

--- a/solution.py
+++ b/solution.py
@@ -19,6 +19,7 @@
 COLS = 1024
 OWN = 16
 PLANE, PLANES = 8, 8
+AGENT = 4
 LENGTH = CTX * ROWS
 VMEM_BYTES = 56 << 20
 
@@ -51,7 +52,7 @@
     hidden, gating, taps, upstream, gain_ref, outer_f32, back_f32, dense_f32, turned_f32, twist_ref,
     outer_ref, back_ref, dense_ref, turned_ref,
     send, recv, spec, part_hi, part_lo, wide, stage, hidden_t, gain_t, sums, sums_in,
-    load_sem, send_sem, recv_sem, sum_send, sum_recv,
+    load_sem, send_sem, recv_sem, sum_send, sum_recv, relay,
 ):
     me, mych = lax.axis_index("ctx"), lax.axis_index("ch")
     plane, place = me // PLANE, lax.rem(me, PLANE)
@@ -84,9 +85,14 @@
     lax.fori_loop(0, PLANES - 1, greet_plane, 0)
     for i in range(1, PLANE):
         greet(plane * PLANE + lax.rem(place + i, PLANE))
-    for i in range(1, CH):
-        peer = lax.rem(mych + i, CH)
-        pl.semaphore_signal(barrier, inc=1, device_id={"ch": peer}, device_id_type=MESH)
+    direct = plane <= AGENT
+
+    def to_channels(semaphore):
+        for i in range(1, CH):
+            peer = lax.rem(mych + i, CH)
+            pl.semaphore_signal(semaphore, inc=1, device_id={"ch": peer}, device_id_type=MESH)
+
+    pl.when(direct)(lambda: to_channels(barrier))
     for load in loads[1:]:
         load.start()
 
@@ -231,16 +237,35 @@
     loads[0].wait()
     for i in blocks:
         turn_out(0, i, taps[:, part(i)[0]].astype(F32))
-    pl.semaphore_wait(barrier, CTX - 1 + CH - 1)
-    exchange(0, lambda block: None)
-
     loads[1].wait()
     partial = jnp.zeros((8, ROWS), F32)
     for i in blocks:
         turned = jnp.transpose(hidden[:, part(i)[0]].astype(F32))
         hidden_t[part(i)[0], :] = turned
         partial = partial + jnp.sum((turned * turned).reshape(16, 8, ROWS), axis=0)
-    add_up(0, partial)
+
+    @pl.when(direct)
+    def _():
+        pl.semaphore_wait(barrier, CTX - 1 + CH - 1)
+        add_up(0, partial)
+
+    @pl.when(plane > AGENT)
+    def _():
+        pl.semaphore_wait(barrier, CTX - 1)
+        agent = AGENT * PLANE + place
+        pl.semaphore_signal(relay.at[0], inc=1, device_id={"ctx": agent}, device_id_type=MESH)
+
+    exchange(0, lambda block: None)
+
+    @pl.when(plane == AGENT)
+    def _():
+        pl.semaphore_wait(relay.at[0], PLANES - 1 - AGENT)
+        to_channels(relay.at[1])
+
+    @pl.when(plane > AGENT)
+    def _():
+        pl.semaphore_wait(relay.at[2], 1)
+        add_up(0, partial)
 
     loads[2].wait()
     loads[3].wait()
@@ -250,6 +275,13 @@
         turn_out(1, block, upstream[:, at].astype(F32) * gating[:, at].astype(F32))
 
     exchange(1, conv_grad)
+
+    @pl.when(plane == AGENT)
+    def _():
+        pl.semaphore_wait(relay.at[1], CH - 1)
+        for later in range(AGENT + 1, PLANES):
+            peer = later * PLANE + place
+            pl.semaphore_signal(relay.at[2], inc=1, device_id={"ctx": peer}, device_id_type=MESH)
 
     loads[4].wait()
     for i in blocks:
@@ -285,7 +317,6 @@
     inverse(2, 0, False)
     exchange(4, from_stage(4))
     inverse(2, 1, True)
-    exchange(5, from_stage(5))
 
     sums[1] = jnp.zeros((8, ROWS), F32)
 
@@ -297,19 +328,20 @@
 
     arrivals(3, project)
     add_up(1, sums[1])
+    exchange(5, from_stage(5))
+
+    def gated(block):
+        at = part(block)[0]
+        value = jnp.transpose(turn_in(4, block))
+        output[:, at] = (gating[:, at].astype(F32) * value).astype(BF16)
+        gate_grad[:, at] = (upstream[:, at].astype(F32) * value).astype(BF16)
+
+    arrivals(4, gated)
     projection = added(1)
     for i in blocks:
         at = part(i)[0]
         value = inverse_rms * (gain_t[at, :] - hidden_t[at, :] * projection)
         hidden_grad[:, at] = jnp.transpose(value).astype(BF16)
-
-    def gated(block):
-        at = part(block)[0]
-        value = jnp.transpose(turn_in(4, block))
-        output[:, at] = (gating[:, at].astype(F32) * value).astype(BF16)
-        gate_grad[:, at] = (upstream[:, at].astype(F32) * value).astype(BF16)
-
-    arrivals(4, gated)
 
     def taps_grad(block):
         filter_grad[:, part(block)[0]] = jnp.transpose(turn_in(5, block)).astype(BF16)
@@ -363,6 +395,7 @@
             pltpu.SemaphoreType.DMA((6, PLANES)),
             pltpu.SemaphoreType.DMA((2,)),
             pltpu.SemaphoreType.DMA((2,)),
+            pltpu.SemaphoreType.REGULAR((3,)),
         ],
         compiler_params=pltpu.CompilerParams(collective_id=0, has_side_effects=True, vmem_limit_bytes=VMEM_BYTES),
     )(hidden, gating, filter_taps, upstream, gain, *consts)

time: 61.6 us -> 59.4 us (0.964)
  Pallas kernels: 60.8 us -> 58.6 us
    pallas_call x1, Pallas kernels: 59.8 us -> 57.6 us  [shards(): pl.pallas_call(kernel, out_shape=(pltpu.VMEM((ROWS, COLS), BF16),) * 4, i...]
where the time goes in v2:
time: 59.4 us; the launch traced here: 59.3 us
  Pallas kernels  58.6 us (99%)
  between operations  0.64 us (1%)
    pallas_call x1, Pallas kernels, shards(): pl.pallas_call(kernel, out_shape=(pltpu.VMEM((ROWS, COLS), BF16),) * 4, i...  57.6 us

profile of v2, /device:TPU:1, one launch (start us, length us, event | category | flops | bytes accessed | tf_op | source)
XLA Modules:
  0.0 59.3 jit_solution(15062514859831108815)
XLA Ops:
  0.6 57.6 %shard_map.129 = (bf16[128,1024]{1,0:T(8,128)(2,1)S(1)}, bf16[128,1024]{1,0:T(8,128)(2,1)S(1)}, bf16[128,1024]{1,0:T(8,128)(2,1)S(1)}, bf16[128,1024]{1,0:T(8,128)(2,1)S(1)}) custom-call(bf16[128,1024]{1,0:T(8,128)(2,1)} %hidden_hbm.1, bf16[128,1024]{1,0:T(8,128)(2,1)} %gating_hbm.1, bf16[128,1024]{1,0:T(8,128)(2,1)} %taps_hbm.1, ...), custom_call_target="tpu_custom_call" | custom-call | tf_op jit(solution)/shard_map/pallas_call | solution.py:370
  58.3 1.0 %shard_map.130 = (bf16[128,1024]{1,0:T(8,128)(2,1)}, bf16[128,1024]{1,0:T(8,128)(2,1)}, bf16[128,1024]{1,0:T(8,128)(2,1)}, bf16[128,1024]{1,0:T(8,128)(2,1)}) custom-call(bf16[128,1024]{1,0:T(8,128)(2,1)S(1)} %get-tuple-element.8.refs_0_, bf16[128,1024]{1,0:T(8,128)(2,1)S(1)} %get-tuple-element.9.refs_1_, bf16[128,1024]{1,0:T(8,128)(2,1)S(1)} %get-tuple-element.10.refs_2_, ...), custom_call_target="tpu_custom_call" | custom-call | tf_op jit(solution)/shard_map/pallas_call | solution.py:402

commit v3 on v2

--- a/solution.py
+++ b/solution.py
@@ -141,9 +141,8 @@
             device_id={"ctx": lax.rem(me + 1, CTX)}, device_id_type=MESH,
         ).wait_send()
 
-    def add_up(which, partial):
-        sums[which] = partial
-        sums_in[which, mych] = partial
+    def add_up(which):
+        sums_in[which, mych] = sums[which]
 
         def one(i, carry):
             peer = lax.rem(mych + i, CH)
@@ -234,26 +233,33 @@
 
     blocks = range(COLS // 128)
 
-    loads[0].wait()
-    for i in blocks:
-        turn_out(0, i, taps[:, part(i)[0]].astype(F32))
-    loads[1].wait()
-    partial = jnp.zeros((8, ROWS), F32)
-    for i in blocks:
-        turned = jnp.transpose(hidden[:, part(i)[0]].astype(F32))
-        hidden_t[part(i)[0], :] = turned
-        partial = partial + jnp.sum((turned * turned).reshape(16, 8, ROWS), axis=0)
+    def turn_filter():
+        loads[0].wait()
+        for i in blocks:
+            turn_out(0, i, taps[:, part(i)[0]].astype(F32))
+
+    def squares():
+        loads[1].wait()
+        partial = jnp.zeros((8, ROWS), F32)
+        for i in blocks:
+            turned = jnp.transpose(hidden[:, part(i)[0]].astype(F32))
+            hidden_t[part(i)[0], :] = turned
+            partial = partial + jnp.sum((turned * turned).reshape(16, 8, ROWS), axis=0)
+        sums[0] = partial
 
     @pl.when(direct)
     def _():
+        turn_filter()
+        squares()
         pl.semaphore_wait(barrier, CTX - 1 + CH - 1)
-        add_up(0, partial)
+        add_up(0)
 
     @pl.when(plane > AGENT)
     def _():
         pl.semaphore_wait(barrier, CTX - 1)
         agent = AGENT * PLANE + place
         pl.semaphore_signal(relay.at[0], inc=1, device_id={"ctx": agent}, device_id_type=MESH)
+        turn_filter()
 
     exchange(0, lambda block: None)
 
@@ -264,8 +270,9 @@
 
     @pl.when(plane > AGENT)
     def _():
+        squares()
         pl.semaphore_wait(relay.at[2], 1)
-        add_up(0, partial)
+        add_up(0)
 
     loads[2].wait()
     loads[3].wait()
@@ -327,7 +334,7 @@
         sums[1] = sums[1] + jnp.sum((scaled * hidden_t[at, :]).reshape(16, 8, ROWS), axis=0)
 
     arrivals(3, project)
-    add_up(1, sums[1])
+    add_up(1)
     exchange(5, from_stage(5))
 
     def gated(block):

time: 59.4 us -> 58.7 us (0.988)
  Pallas kernels: 58.6 us -> 57.9 us
    pallas_call x1, Pallas kernels: 57.6 us -> 56.9 us  [shards(): pl.pallas_call(kernel, out_shape=(pltpu.VMEM((ROWS, COLS), BF16),) * 4, i...]
where the time goes in v3:
time: 58.7 us; the launch traced here: 58.5 us
  Pallas kernels  57.9 us (99%)
  between operations  0.64 us (1%)
    pallas_call x1, Pallas kernels, shards(): pl.pallas_call(kernel, out_shape=(pltpu.VMEM((ROWS, COLS), BF16),) * 4, i...  56.9 us

profile of v3, /device:TPU:1, one launch (start us, length us, event | category | flops | bytes accessed | tf_op | source)
XLA Modules:
  0.0 58.5 jit_solution(2070148857738388420)
XLA Ops:
  0.6 56.9 %shard_map.129 = (bf16[128,1024]{1,0:T(8,128)(2,1)S(1)}, bf16[128,1024]{1,0:T(8,128)(2,1)S(1)}, bf16[128,1024]{1,0:T(8,128)(2,1)S(1)}, bf16[128,1024]{1,0:T(8,128)(2,1)S(1)}) custom-call(bf16[128,1024]{1,0:T(8,128)(2,1)} %hidden_hbm.1, bf16[128,1024]{1,0:T(8,128)(2,1)} %gating_hbm.1, bf16[128,1024]{1,0:T(8,128)(2,1)} %taps_hbm.1, ...), custom_call_target="tpu_custom_call" | custom-call | tf_op jit(solution)/shard_map/pallas_call | solution.py:377
  57.5 1.0 %shard_map.130 = (bf16[128,1024]{1,0:T(8,128)(2,1)}, bf16[128,1024]{1,0:T(8,128)(2,1)}, bf16[128,1024]{1,0:T(8,128)(2,1)}, bf16[128,1024]{1,0:T(8,128)(2,1)}) custom-call(bf16[128,1024]{1,0:T(8,128)(2,1)S(1)} %get-tuple-element.8.refs_0_, bf16[128,1024]{1,0:T(8,128)(2,1)S(1)} %get-tuple-element.9.refs_1_, bf16[128,1024]{1,0:T(8,128)(2,1)S(1)} %get-tuple-element.10.refs_2_, ...), custom_call_target="tpu_custom_call" | custom-call | tf_op jit(solution)/shard_map/pallas_call | solution.py:409

commit v4 on v3

--- a/solution.py
+++ b/solution.py
@@ -294,16 +294,6 @@
     for i in blocks:
         at = part(i)[0]
         gain_t[at, :] = jnp.transpose(jnp.broadcast_to(gain_ref[:, at], (ROWS, 128)))
-    inverse_rms = lax.rsqrt(added(0) + EPSILON)
-
-    def mixed(block):
-        at, owners = part(block)
-        normed = hidden_t[at, :] * inverse_rms
-        hidden_t[at, :] = normed
-        send[2, owners] = (normed * gain_t[at, :]).astype(BF16).reshape(PLANE, OWN, ROWS)
-
-    exchange(2, mixed)
-
     for load in loads[5:]:
         load.wait()
     high, low = split(outer_f32[...])
@@ -315,6 +305,16 @@
 
     arrivals(0, to_stage(0))
     forward(0)
+    inverse_rms = lax.rsqrt(added(0) + EPSILON)
+
+    def mixed(block):
+        at, owners = part(block)
+        normed = hidden_t[at, :] * inverse_rms
+        hidden_t[at, :] = normed
+        send[2, owners] = (normed * gain_t[at, :]).astype(BF16).reshape(PLANE, OWN, ROWS)
+
+    exchange(2, mixed)
+
     arrivals(1, to_stage(1))
     forward(1)
     inverse(0, 1, True)

time: 58.7 us -> 59.5 us (1.014)
  Pallas kernels: 57.9 us -> 58.7 us
    pallas_call x1, Pallas kernels: 56.9 us -> 57.7 us  [shards(): pl.pallas_call(kernel, out_shape=(pltpu.VMEM((ROWS, COLS), BF16),) * 4, i...]
where the time goes in v4:
time: 59.5 us; the launch traced here: 59.3 us
  Pallas kernels  58.7 us (99%)
  between operations  0.64 us (1%)
    pallas_call x1, Pallas kernels, shards(): pl.pallas_call(kernel, out_shape=(pltpu.VMEM((ROWS, COLS), BF16),) * 4, i...  57.7 us

profile of v4, /device:TPU:1, one launch (start us, length us, event | category | flops | bytes accessed | tf_op | source)
XLA Modules:
  0.0 59.3 jit_solution(13586012033925072112)
XLA Ops:
  0.6 57.7 %shard_map.129 = (bf16[128,1024]{1,0:T(8,128)(2,1)S(1)}, bf16[128,1024]{1,0:T(8,128)(2,1)S(1)}, bf16[128,1024]{1,0:T(8,128)(2,1)S(1)}, bf16[128,1024]{1,0:T(8,128)(2,1)S(1)}) custom-call(bf16[128,1024]{1,0:T(8,128)(2,1)} %hidden_hbm.1, bf16[128,1024]{1,0:T(8,128)(2,1)} %gating_hbm.1, bf16[128,1024]{1,0:T(8,128)(2,1)} %taps_hbm.1, ...), custom_call_target="tpu_custom_call" | custom-call | tf_op jit(solution)/shard_map/pallas_call | solution.py:377
  58.3 1.0 %shard_map.130 = (bf16[128,1024]{1,0:T(8,128)(2,1)}, bf16[128,1024]{1,0:T(8,128)(2,1)}, bf16[128,1024]{1,0:T(8,128)(2,1)}, bf16[128,1024]{1,0:T(8,128)(2,1)}) custom-call(bf16[128,1024]{1,0:T(8,128)(2,1)S(1)} %get-tuple-element.8.refs_0_, bf16[128,1024]{1,0:T(8,128)(2,1)S(1)} %get-tuple-element.9.refs_1_, bf16[128,1024]{1,0:T(8,128)(2,1)S(1)} %get-tuple-element.10.refs_2_, ...), custom_call_target="tpu_custom_call" | custom-call | tf_op jit(solution)/shard_map/pallas_call | solution.py:409
